TPU v7x, 32 devices: a whole 2x2x4 slice. The times are simulated.
32 devices in a mesh: pool: 2 (over x), row: 8 (over z, y), col: 2 (over core).
Axes of the slice: x: 2, y: 2, z: 4, core: 2. Of those that a mesh axis runs over, the one named last changes fastest.
Arguments:
- row_features: bfloat16 [128, 32768], P('col', ('pool', 'row')), parts along dimension 1, may hold values from -6 to 6
- col_features: bfloat16 [128, 16384], P('row', ('pool', 'col')), parts along dimension 1, may hold values from -6 to 6
- solve_rows: float32 [32768], P(('pool', 'row')), parts along dimension 0, may hold values from -16 to 16
- solve_cols: float32 [16384], P(('pool', 'col')), parts along dimension 0, may hold values from -16 to 16
- probe_rows: float32 [16, 32768], P(None, ('pool', 'row')), parts along dimension 1, may hold values from -16 to 16
- probe_cols: float32 [16, 16384], P(None, ('pool', 'col')), parts along dimension 1, may hold values from -12 to 12
Outputs:
- row_grad: float32 [128, 32768], P('col', ('pool', 'row')), parts along dimension 1
- col_grad: float32 [128, 16384], P('row', ('pool', 'col')), parts along dimension 1
There are 2 independent parts, one for each index of `pool`. A program takes and returns all parts, laid end to end along the dimension named above; each array names one. Nothing has to cross between parts.
All inputs are finite; a program needn't handle non-finite values.
Results may differ from a plain program's by a relative error of at most 0.0022.
Values may be sent and summed in bfloat16 or wider, within the bound.
A program may use at most 64 MiB of HBM per device.

v0:
```python
import jax
import jax.numpy as jnp
from jax import lax
from jax.sharding import PartitionSpec as P

FEATURES = 128
PROBES = 16


def outer_sum(p_weight, q_weight):
    total = p_weight[0][:, None] * q_weight[0][None, :]
    for index_now in range(1, p_weight.shape[0]):
        total = total + p_weight[index_now][:, None] * q_weight[index_now][None, :]
    return total


def tile_terms(p_feat, p_norm, q_feat, p_weight, q_weight, inverse_sq):
    q_wide = q_feat.astype(jnp.float32)
    cross_term = lax.dot_general(
        p_feat, q_feat, (((0,), (0,)), ((), ())), preferred_element_type=jnp.float32
    )
    sq_dist = p_norm[:, None] + jnp.sum(q_wide * q_wide, 0)[None, :] - 2.0 * cross_term
    kernel_tile = jnp.exp(-0.5 * inverse_sq * sq_dist)
    coupling = outer_sum(p_weight, q_weight)
    weighted = coupling * kernel_tile
    weighted_bf = weighted.astype(jnp.bfloat16)
    p_part = lax.dot_general(
        q_feat, weighted_bf, (((1,), (1,)), ((), ())), preferred_element_type=jnp.float32
    )
    q_part = lax.dot_general(
        p_feat, weighted_bf, (((1,), (0,)), ((), ())), preferred_element_type=jnp.float32
    )
    q_grad = inverse_sq * (q_part - q_wide * jnp.sum(weighted, 0)[None, :])
    return (p_part, jnp.sum(weighted, 1), q_grad)


def unchanged(values):
    return values


def sweep_tiles(p_feat, fetch_cols, p_weight, q_weight, finish, out_rows, inverse_sq):
    p_wide = p_feat.astype(jnp.float32)
    p_norm = jnp.sum(p_wide * p_wide, 0)
    p_count = p_feat.shape[1]
    q_count = q_weight.shape[1]
    block_size = min(q_count, max(1024, 2097152 // p_count))

    def one_turn(index_now, state_now):
        p_sum, row_sum, stored = state_now
        col_start = index_now * block_size
        q_feat = fetch_cols(col_start, block_size)
        q_slice = lax.dynamic_slice_in_dim(q_weight, col_start, block_size, 1)
        p_part, row_part, q_grad = tile_terms(p_feat, p_norm, q_feat, p_weight, q_slice, inverse_sq)
        stored = lax.dynamic_update_slice_in_dim(stored, finish(q_grad), col_start, 1)
        return (p_sum + p_part, row_sum + row_part, stored)

    initial = (
        jnp.zeros((p_feat.shape[0], p_count), jnp.float32),
        jnp.zeros((p_count,), jnp.float32),
        jnp.zeros((out_rows, q_count), jnp.float32),
    )
    p_sum, row_sum, stored = lax.fori_loop(0, q_count // block_size, one_turn, initial)
    return (inverse_sq * (p_sum - p_wide * row_sum[None, :]), stored)


def shards(row_features, col_features, solve_rows, solve_cols, probe_rows, probe_cols):
    inverse_sq = 4.0 / FEATURES
    row_weight = jnp.concatenate([0.5 * solve_rows[None, :], -0.5 / PROBES * probe_rows], 0)
    col_weight = jnp.concatenate([solve_cols[None, :], probe_cols], 0)
    row_full = lax.all_gather(row_features, "col", axis=0, tiled=True)
    col_full = lax.all_gather(col_features, "row", axis=0, tiled=True)

    def fetch_cols(col_start, col_count):
        return lax.dynamic_slice_in_dim(col_full, col_start, col_count, 1)

    row_part, col_store = sweep_tiles(
        row_full, fetch_cols, row_weight, col_weight, unchanged, FEATURES, inverse_sq
    )
    col_grad = lax.psum_scatter(col_store, "row", scatter_dimension=0, tiled=True)
    row_grad = lax.psum_scatter(row_part, "col", scatter_dimension=0, tiled=True)
    return (row_grad, col_grad)


def solution(mesh):
    return jax.shard_map(
        shards,
        mesh=mesh,
        in_specs=(
            P("col", ("pool", "row")),
            P("row", ("pool", "col")),
            P(("pool", "row")),
            P(("pool", "col")),
            P(None, ("pool", "row")),
            P(None, ("pool", "col")),
        ),
        out_specs=(P("col", ("pool", "row")), P("row", ("pool", "col"))),
        check_vma=False,
    )
```

profile of v0, /device:TPU:0, one launch (start us, length us, event | category | flops | bytes accessed | tf_op | source)
XLA Modules:
  0.0 237.2 jit_solution(16441979207571882287)
XLA Ops:
  7.2 0.0 all-gather.2.cloned.1.call-start
  7.2 0.7 all-gather.2.cloned.1.call-update
  7.9 0.0 reduce-scatter.3.cloned.1.call-start
  8.0 2.5 %all_gather.7 = bf16[128,2048]{1,0:T(8,128)(2,1)S(1)} all-gather(bf16[64,2048]{1,0:T(8,128)(2,1)} %param.8), channel_id=1, replica_groups=mesh['pool'=2,'row'=8,'col'=2] {'col'}, dimensions={0}, use_global_device_ids=true | all-gather | bytes 786432 | tf_op jit(solution)/shard_map/all_gather | solution.py:70
  10.4 0.1 fusion.16
  10.6 0.7 broadcast_multiply_fusion.1
  11.3 0.9 broadcast_multiply_fusion
  12.2 1.0 pad_maximum_fusion
  13.2 39.8 %all-gather.2.cloned.1.call-done = bf16[128,4096]{1,0:T(8,128)(2,1)} async-done(((bf16[16,4096]{1,0:T(8,128)(2,1)}), bf16[128,4096]{1,0:T(8,128)(2,1)}) %all-gather.2.cloned.1.call-update) | async-done | bytes 1048592 | tf_op jit(solution)/shard_map/all_gather | solution.py:71
  53.0 1.5 broadcast_in_dim.25.clone
  54.5 94.0 %while.18 = (s32[]{:T(128)}, f32[128,2048]{1,0:T(8,128)S(1)}, f32[2048]{0:T(1024)S(1)}, f32[128,4096]{1,0:T(8,128)}, bf16[128,4096]{1,0:T(8,128)(2,1)}, /*index=...) while((s32[]{:T(128)}, f32[128,2048]{1,0:T(8,128)S(1)}, ...), condition=%wide.region_5.0_spmd.clone, body=%wide.region_1.0_spmd.clone.sunk | while | flops 1698037760 | bytes 37892716 | solution.py:62
  54.5 1.0 constant_dynamic-slice_fusion.4
  55.5 0.2 copy.18
  55.7 0.2 fusion.43
  55.9 0.3 constant_dynamic-slice_fusion.5
  56.2 0.1 fusion.44
  56.3 16.0 %fusion.45 = (f32[1024]{0:T(1024)S(1)}, f32[2048]{0:T(1024)S(1)}, bf16[2048,1024]{0,1:T(8,128)(2,1)}) fusion(bf16[128,1024]{1,0:T(8,128)(2,1)S(1)} %constant_dynamic-slice_fusion.4, bf16[128,2048]{1,0:T(8,128)(2,1)S(1)} %get-tuple-element.480, f32[1024]{0:T(1024)S(1)} %fusion.43, f32[2048]{0:T(1024)S(1)} %get-tuple-element.479, ...), kind=kOutput, calls=%fused_computation.26.clone.1 | convolution fusion | flops 622851072 | bytes 5214208 | tf_op jit(solution)/shard_map/while/body/eval_jaxpr/dot_general | solution.py:19
  72.3 0.0 copy-start
  72.3 3.3 %convolution_add_fusion.2 = f32[128,2048]{1,0:T(8,128)S(1)} fusion(bf16[128,1024]{1,0:T(8,128)(2,1)S(1)} %constant_dynamic-slice_fusion.4, bf16[2048,1024]{0,1:T(8,128)(2,1)} %get-tuple-element.408, f32[128,2048]{1,0:T(8,128)S(1)} %get-tuple-element.442, pred[]{:T(512)S(6)} %compare.3), kind=kOutput, calls=%fused_computation.4.clone.1 | convolution fusion | flops 537395200 | bytes 6553601 | tf_op jit(solution)/shard_map/while/body/eval_jaxpr/dot_general | solution.py:27
  75.6 0.1 copy-done
  75.8 1.3 fusion.46
  77.0 0.2 copy.19
  77.2 0.8 constant_dynamic-update-slice_fusion.2
  78.0 1.0 constant_dynamic-slice_fusion.4
  79.0 0.2 copy.18
  79.2 0.2 fusion.43
  79.4 0.3 constant_dynamic-slice_fusion.5
  79.7 0.1 fusion.44
  79.8 16.0 %fusion.45 = (f32[1024]{0:T(1024)S(1)}, f32[2048]{0:T(1024)S(1)}, bf16[2048,1024]{0,1:T(8,128)(2,1)}) fusion(bf16[128,1024]{1,0:T(8,128)(2,1)S(1)} %constant_dynamic-slice_fusion.4, bf16[128,2048]{1,0:T(8,128)(2,1)S(1)} %get-tuple-element.480, f32[1024]{0:T(1024)S(1)} %fusion.43, f32[2048]{0:T(1024)S(1)} %get-tuple-element.479, ...), kind=kOutput, calls=%fused_computation.26.clone.1 | convolution fusion | flops 622851072 | bytes 5214208 | tf_op jit(solution)/shard_map/while/body/eval_jaxpr/dot_general | solution.py:19
  95.8 3.3 %convolution_add_fusion.2 = f32[128,2048]{1,0:T(8,128)S(1)} fusion(bf16[128,1024]{1,0:T(8,128)(2,1)S(1)} %constant_dynamic-slice_fusion.4, bf16[2048,1024]{0,1:T(8,128)(2,1)} %get-tuple-element.408, f32[128,2048]{1,0:T(8,128)S(1)} %get-tuple-element.442, pred[]{:T(512)S(6)} %compare.3), kind=kOutput, calls=%fused_computation.4.clone.1 | convolution fusion | flops 537395200 | bytes 6553601 | tf_op jit(solution)/shard_map/while/body/eval_jaxpr/dot_general | solution.py:27
  99.1 0.1 copy-done
  99.2 1.3 fusion.46
  100.5 0.2 copy.19
  100.7 0.9 constant_dynamic-update-slice_fusion.2
  101.6 1.0 constant_dynamic-slice_fusion.4
  102.5 0.2 copy.18
  102.7 0.2 fusion.43
  102.9 0.3 constant_dynamic-slice_fusion.5
  103.2 0.1 fusion.44
  103.3 16.0 %fusion.45 = (f32[1024]{0:T(1024)S(1)}, f32[2048]{0:T(1024)S(1)}, bf16[2048,1024]{0,1:T(8,128)(2,1)}) fusion(bf16[128,1024]{1,0:T(8,128)(2,1)S(1)} %constant_dynamic-slice_fusion.4, bf16[128,2048]{1,0:T(8,128)(2,1)S(1)} %get-tuple-element.480, f32[1024]{0:T(1024)S(1)} %fusion.43, f32[2048]{0:T(1024)S(1)} %get-tuple-element.479, ...), kind=kOutput, calls=%fused_computation.26.clone.1 | convolution fusion | flops 622851072 | bytes 5214208 | tf_op jit(solution)/shard_map/while/body/eval_jaxpr/dot_general | solution.py:19
  119.3 0.0 copy-start
  119.3 3.3 %convolution_add_fusion.2 = f32[128,2048]{1,0:T(8,128)S(1)} fusion(bf16[128,1024]{1,0:T(8,128)(2,1)S(1)} %constant_dynamic-slice_fusion.4, bf16[2048,1024]{0,1:T(8,128)(2,1)} %get-tuple-element.408, f32[128,2048]{1,0:T(8,128)S(1)} %get-tuple-element.442, pred[]{:T(512)S(6)} %compare.3), kind=kOutput, calls=%fused_computation.4.clone.1 | convolution fusion | flops 537395200 | bytes 6553601 | tf_op jit(solution)/shard_map/while/body/eval_jaxpr/dot_general | solution.py:27
  122.6 0.1 copy-done
  122.8 1.3 fusion.46
  124.0 0.2 copy.19
  124.2 0.8 constant_dynamic-update-slice_fusion.2
  125.1 1.0 constant_dynamic-slice_fusion.4
  126.0 0.2 copy.18
  126.2 0.2 fusion.43
  126.4 0.3 constant_dynamic-slice_fusion.5
  126.7 0.1 fusion.44
  126.8 16.0 %fusion.45 = (f32[1024]{0:T(1024)S(1)}, f32[2048]{0:T(1024)S(1)}, bf16[2048,1024]{0,1:T(8,128)(2,1)}) fusion(bf16[128,1024]{1,0:T(8,128)(2,1)S(1)} %constant_dynamic-slice_fusion.4, bf16[128,2048]{1,0:T(8,128)(2,1)S(1)} %get-tuple-element.480, f32[1024]{0:T(1024)S(1)} %fusion.43, f32[2048]{0:T(1024)S(1)} %get-tuple-element.479, ...), kind=kOutput, calls=%fused_computation.26.clone.1 | convolution fusion | flops 622851072 | bytes 5214208 | tf_op jit(solution)/shard_map/while/body/eval_jaxpr/dot_general | solution.py:19
  142.8 0.0 copy-start
  142.8 3.3 %convolution_add_fusion.2 = f32[128,2048]{1,0:T(8,128)S(1)} fusion(bf16[128,1024]{1,0:T(8,128)(2,1)S(1)} %constant_dynamic-slice_fusion.4, bf16[2048,1024]{0,1:T(8,128)(2,1)} %get-tuple-element.408, f32[128,2048]{1,0:T(8,128)S(1)} %get-tuple-element.442, pred[]{:T(512)S(6)} %compare.3), kind=kOutput, calls=%fused_computation.4.clone.1 | convolution fusion | flops 537395200 | bytes 6553601 | tf_op jit(solution)/shard_map/while/body/eval_jaxpr/dot_general | solution.py:27
  146.1 0.1 copy-done
  146.3 1.3 fusion.46
  147.5 0.2 copy.19
  147.7 0.9 constant_dynamic-update-slice_fusion.2
  148.6 1.2 fusion.18
  149.8 0.0 reduce-scatter.3.cloned.1.call-update
  149.8 0.0 reduce-scatter.5.cloned.1.call-start
  149.8 0.7 reduce-scatter.5.cloned.1.call-update
  150.5 6.7 %reduce-scatter.3.cloned.1.call-done = f32[64,2048]{1,0:T(8,128)} async-done(((f32[128,2048]{1,0:T(8,128)}), f32[64,2048]{1,0:T(8,128)}) %reduce-scatter.3.cloned.1.call-update) | async-done | bytes 524304 | tf_op jit(solution)/shard_map/reduce_scatter | solution.py:80
  157.2 73.5 %reduce-scatter.5.cloned.1.call-done = f32[16,4096]{1,0:T(8,128)} async-done(((f32[128,4096]{1,0:T(8,128)}), f32[16,4096]{1,0:T(8,128)}) %reduce-scatter.5.cloned.1.call-update) | async-done | bytes 262160 | tf_op jit(solution)/shard_map/reduce_scatter | solution.py:79
  (7 shorter events, 0.0 us)
Async XLA Ops:
  7.2 45.8 %all-gather.2.cloned.1.call-start = ((), (), s32[]{:S(2)}) async-start(), calls=%async_computation.2 | async-start | bytes 1179648 | tf_op jit(solution)/shard_map/all_gather | solution.py:71
  7.9 149.3 %reduce-scatter.3.cloned.1.call-start = ((), (), s32[]{:S(2)}) async-start(), calls=%async_computation.3 | async-start | bytes 1572864 | tf_op jit(solution)/shard_map/reduce_scatter | solution.py:80
  72.3 3.4 %copy-start = (bf16[2048,1024]{0,1:T(8,128)(2,1)S(1)}, bf16[2048,1024]{0,1:T(8,128)(2,1)}, u32[]{:S(2)}) copy-start(bf16[2048,1024]{0,1:T(8,128)(2,1)} %get-tuple-element.408) | copy-start | bytes 12582916 | tf_op jit(solution)/shard_map/while
  95.8 3.4 %copy-start = (bf16[2048,1024]{0,1:T(8,128)(2,1)S(1)}, bf16[2048,1024]{0,1:T(8,128)(2,1)}, u32[]{:S(2)}) copy-start(bf16[2048,1024]{0,1:T(8,128)(2,1)} %get-tuple-element.408) | copy-start | bytes 12582916 | tf_op jit(solution)/shard_map/while
  119.3 3.4 %copy-start = (bf16[2048,1024]{0,1:T(8,128)(2,1)S(1)}, bf16[2048,1024]{0,1:T(8,128)(2,1)}, u32[]{:S(2)}) copy-start(bf16[2048,1024]{0,1:T(8,128)(2,1)} %get-tuple-element.408) | copy-start | bytes 12582916 | tf_op jit(solution)/shard_map/while
  142.8 3.4 %copy-start = (bf16[2048,1024]{0,1:T(8,128)(2,1)S(1)}, bf16[2048,1024]{0,1:T(8,128)(2,1)}, u32[]{:S(2)}) copy-start(bf16[2048,1024]{0,1:T(8,128)(2,1)} %get-tuple-element.408) | copy-start | bytes 12582916 | tf_op jit(solution)/shard_map/while
  149.8 80.9 %reduce-scatter.5.cloned.1.call-start = ((), (), s32[]{:S(2)}) async-start(), calls=%async_computation.4 | async-start | bytes 2359296 | tf_op jit(solution)/shard_map/reduce_scatter | solution.py:79
Sparse Core Ops, SparseCore 0:
  10.1 42.8 all-gather.1
  149.9 7.2 reduce-scatter.2
  161.8 68.8 reduce-scatter.4
where the time goes:
time: 238 us; the launch traced here: 237 us
  waiting for transfers between devices  121 us (51%)
  matrix products  82.3 us (35%)
  between operations  13.8 us (6%)
  local copies, waits for them, and re-layouts  12.2 us (5%)
  other arithmetic  4.77 us (2%)
  blocking collectives  2.47 us (1%)
    reduce_scatter x1, waiting for transfers between devices, shards(): lax.psum_scatter(col_store, 'row', scatter_dimension=0, tiled=True)  73.5 us
    dot_general x4, matrix products, tile_terms(): lax.dot_general(p_feat, q_feat, (((0,), (0,)), ((), ())), preferred_eleme...  64.1 us
    all_gather x1, waiting for transfers between devices, shards(): col_full = lax.all_gather(col_features, 'row', axis=0, tiled=True)  39.8 us
    dot_general x4, matrix products, tile_terms(): lax.dot_general(q_feat, weighted_bf, (((1,), (1,)), ((), ())), preferred_...  13.1 us
    reduce_scatter x1, waiting for transfers between devices, shards(): lax.psum_scatter(row_part, 'col', scatter_dimension=0, tiled=True)  6.72 us
    dot_general x4, matrix products, tile_terms(): lax.dot_general(p_feat, weighted_bf, (((1,), (0,)), ((), ())), preferred_...  5.02 us
  transfers between devices with their start and end apart: 3, of which 3 were waited for; matrix products, arithmetic and copies ran while one was open for 1% of the time, Pallas kernels for 0%

commit v1 on v0

v1 whole, which is shorter than its diff:
```python
import functools

import jax
import jax.numpy as jnp
from jax import lax
from jax.experimental import pallas as pl
from jax.experimental.pallas import tpu as pltpu
from jax.sharding import PartitionSpec as P

FEATURES = 128
PROBES = 16
WIDE = FEATURES + 16
WEIGHT_ROWS = 64
STRIP = 512
ROW_TILE = 256
COL_TILE = 512
LOG2E = 1.4426950408889634
F32 = jnp.float32
BF16 = jnp.bfloat16


def split_parts(values, count):
    parts = []
    for _ in range(count - 1):
        high = values.astype(BF16).astype(F32)
        parts.append(high)
        values = values - high
    parts.append(values)
    return parts


def half_norm(features):
    wide = features.astype(F32)
    return jnp.concatenate(split_parts(-0.5 * jnp.sum(wide * wide, 0, keepdims=True), 3), 0)


def extra_rows(features, norm_first):
    count = features.shape[1]
    ones = jnp.ones((3, count), F32)
    pad = jnp.zeros((WIDE - FEATURES - 6, count), F32)
    norm = half_norm(features)
    rows = [norm, ones, pad] if norm_first else [ones, norm, pad]
    return jnp.concatenate(rows, 0).astype(BF16)


def weight_rows(solve, probe, solve_scale, probe_scale, low_last):
    high, low = split_parts(jnp.concatenate([solve_scale * solve, probe_scale * probe], 0), 2)
    pad = jnp.zeros((WEIGHT_ROWS - 3 * (PROBES + 1), solve.shape[1]), F32)
    parts = [high, high, low] if low_last else [high, low, high]
    return jnp.concatenate(parts + [pad], 0).astype(BF16)


def window(index_now, size):
    return pl.ds(pl.multiple_of(index_now * size, size), size)


def turned(values):
    return values.astype(F32).T.astype(BF16)


def local_kernel(
    x_ref, z_ref, sr_ref, sc_ref, pr_ref, pc_ref, row_ref, col_ref,
    x_aug, z_aug, x_turn, rw_turn, c_weight, row_acc, col_acc,
):
    inverse_sq = 4.0 / FEATURES
    row_count, col_count = x_ref.shape[1], z_ref.shape[1]
    row_tiles = row_count // ROW_TILE

    @pl.loop(0, row_count // STRIP)
    def _(index_now):
        at = window(index_now, STRIP)
        x = x_ref[:, at]
        x_aug[0:FEATURES, at] = x
        x_aug[FEATURES:WIDE, at] = extra_rows(x, False)
        x_turn[at, :] = turned(x_aug[:, at])
        rw_turn[at, :] = turned(weight_rows(sr_ref[:, at], pr_ref[:, at], 0.5, -0.5 / PROBES, False))

    @pl.loop(0, col_count // STRIP)
    def _(index_now):
        at = window(index_now, STRIP)
        z = z_ref[:, at]
        z_aug[0:FEATURES, at] = z
        z_aug[FEATURES:WIDE, at] = extra_rows(z, True)
        c_weight[:, at] = weight_rows(sc_ref[:, at], pc_ref[:, at], 1.0, 1.0, True)

    row_acc[...] = jnp.zeros_like(row_acc)

    def weighted_tile(i, at_j):
        at_i = pl.ds(i * ROW_TILE, ROW_TILE)
        half = jnp.dot(x_turn[at_i, :], z_aug[:, at_j], preferred_element_type=F32)
        coupling = jnp.dot(rw_turn[at_i, :], c_weight[:, at_j], preferred_element_type=F32)
        return (coupling * jnp.exp2(half * (inverse_sq * LOG2E))).astype(BF16)

    @pl.loop(0, col_count // COL_TILE)
    def _(j):
        at_j = window(j, COL_TILE)
        weighted = weighted_tile(0, at_j)
        for i in range(row_tiles):
            following = weighted_tile(i + 1, at_j) if i + 1 < row_tiles else None
            at_i = pl.ds(i * ROW_TILE, ROW_TILE)
            row_acc[:, at_i] += lax.dot_general(
                z_aug[:, at_j], weighted, (((1,), (1,)), ((), ())), preferred_element_type=F32
            )
            part = jnp.dot(x_aug[:, at_i], weighted, preferred_element_type=F32)
            if i == 0:
                col_acc[...] = part
            else:
                col_acc[...] += part
            weighted = following
        col_ref[:, at_j] = inverse_sq * (
            col_acc[0:FEATURES, :] - z_ref[:, at_j].astype(F32) * col_acc[FEATURES:FEATURES + 1, :]
        )

    @pl.loop(0, row_count // STRIP)
    def _(index_now):
        at = window(index_now, STRIP)
        row_ref[:, at] = inverse_sq * (
            row_acc[0:FEATURES, at] - x_ref[:, at].astype(F32) * row_acc[FEATURES + 3:FEATURES + 4, at]
        )


def shards(row_features, col_features, solve_rows, solve_cols, probe_rows, probe_cols):
    row_count, col_count = row_features.shape[1], col_features.shape[1]
    row_full = lax.all_gather(row_features, "col", axis=0, tiled=True)
    col_full = lax.all_gather(col_features, "row", axis=0, tiled=True)
    vmem = pl.BlockSpec(memory_space=pltpu.VMEM)
    row_part, col_part = pl.pallas_call(
        local_kernel,
        out_shape=(
            jax.ShapeDtypeStruct((FEATURES, row_count), F32),
            jax.ShapeDtypeStruct((FEATURES, col_count), F32),
        ),
        in_specs=[vmem] * 6,
        out_specs=(vmem, vmem),
        scratch_shapes=[
            pltpu.VMEM((WIDE, row_count), BF16),
            pltpu.VMEM((WIDE, col_count), BF16),
            pltpu.VMEM((row_count, WIDE), BF16),
            pltpu.VMEM((row_count, WEIGHT_ROWS), BF16),
            pltpu.VMEM((WEIGHT_ROWS, col_count), BF16),
            pltpu.VMEM((WIDE, row_count), F32),
            pltpu.VMEM((WIDE, COL_TILE), F32),
        ],
        compiler_params=pltpu.CompilerParams(vmem_limit_bytes=48 * 2**20),
        name="local_sweep",
    )(row_full, col_full, solve_rows[None, :], solve_cols[None, :], probe_rows, probe_cols)
    col_grad = lax.psum_scatter(col_part, "row", scatter_dimension=0, tiled=True)
    row_grad = lax.psum_scatter(row_part, "col", scatter_dimension=0, tiled=True)
    return (row_grad, col_grad)


def solution(mesh):
    return jax.shard_map(
        shards,
        mesh=mesh,
        in_specs=(
            P("col", ("pool", "row")),
            P("row", ("pool", "col")),
            P(("pool", "row")),
            P(("pool", "col")),
            P(None, ("pool", "row")),
            P(None, ("pool", "col")),
        ),
        out_specs=(P("col", ("pool", "row")), P("row", ("pool", "col"))),
        check_vma=False,
    )
```

time: 238 us -> 165 us (0.69)
  matrix products: 82.3 us -> 0 us
  Pallas kernels: 0 us -> 19.8 us
  local copies, waits for them, and re-layouts: 12.2 us -> 4.49 us
  other arithmetic: 4.77 us -> 0 us
  waiting for transfers between devices: 121 us -> 124 us
    dot_general x12 -> x0, matrix products: 82.3 us -> none  [the longest x4 64.1 us: tile_terms(): lax.dot_general(p_feat, q_feat, (((0,), (0,)), ((), ())), preferred_eleme...]
    pallas_call x0 -> x1, Pallas kernels: none -> 19.8 us  [shards(): pl.pallas_call(local_kernel, out_shape=(jax.ShapeDtypeStruct((FEATURES, r...]
    dynamic_slice x8 -> x0, local copies, waits for them, and re-layouts: 4.54 us -> none  [fetch_cols(): return lax.dynamic_slice_in_dim(col_full, col_start, col_count, 1)]
    unnamed x0 -> x10, local copies, waits for them, and re-layouts: none -> 4.49 us
    dynamic_update_slice x8 -> x0, local copies, waits for them, and re-layouts: 4.16 us -> none  [one_turn(): lax.dynamic_update_slice_in_dim(stored, finish(q_grad), col_start, 1)]
    mul x3 -> x0, other arithmetic: 2.77 us -> none  [the longest x1 1.15 us: sweep_tiles(): return (inverse_sq * (p_sum - p_wide * row_sum[None, :]), stored)]
    all_gather x1, waiting for transfers between devices: 39.8 us -> 42.6 us  [shards(): col_full = lax.all_gather(col_features, 'row', axis=0, tiled=True)]
  transfers between devices with their start and end apart: 3 -> 3, of which waited for: 3 -> 3; matrix products, arithmetic and copies ran while one was open for 1% -> 0% of each run, Pallas kernels for 0% -> 0%
where the time goes in v1:
time: 165 us
  waiting for transfers between devices  124 us (75%)
  Pallas kernels  19.8 us (12%)
  between operations  13.7 us (8%)
  local copies, waits for them, and re-layouts  4.49 us (3%)
  blocking collectives  2.47 us (1%)
    reduce_scatter x1, waiting for transfers between devices, shards(): lax.psum_scatter(col_part, 'row', scatter_dimension=0, tiled=True)  73.6 us
    all_gather x1, waiting for transfers between devices, shards(): col_full = lax.all_gather(col_features, 'row', axis=0, tiled=True)  42.6 us
    pallas_call x1, Pallas kernels, shards(): pl.pallas_call(local_kernel, out_shape=(jax.ShapeDtypeStruct((FEATURES, r...  19.8 us
    reduce_scatter x1, waiting for transfers between devices, shards(): lax.psum_scatter(row_part, 'col', scatter_dimension=0, tiled=True)  6.72 us
    unnamed x10, local copies, waits for them, and re-layouts  4.49 us
  transfers between devices with their start and end apart: 3, of which 3 were waited for; matrix products, arithmetic and copies ran while one was open for 0% of the time, Pallas kernels for 0%

profile of v1, /device:TPU:0, one launch (start us, length us, event | category | flops | bytes accessed | tf_op | source)
XLA Modules:
  0.0 164.9 jit_solution(6394594649290285634)
XLA Ops:
  7.2 0.0 all-gather.2.cloned.1.call-start
  7.2 0.7 all-gather.2.cloned.1.call-update
  7.9 0.0 reduce-scatter.3.cloned.1.call-start
  7.9 2.5 %all_gather.6.x_ref = bf16[128,2048]{1,0:T(8,128)(2,1)S(1)} all-gather(bf16[64,2048]{1,0:T(8,128)(2,1)} %param.6), channel_id=1, replica_groups=mesh['pool'=2,'row'=8,'col'=2] {'col'}, dimensions={0}, use_global_device_ids=true | all-gather | bytes 786432 | tf_op jit(solution)/shard_map/all_gather | solution.py:124
  10.4 42.6 %all-gather.2.cloned.1.call-done.z_ref = bf16[128,4096]{1,0:T(8,128)(2,1)} async-done(((bf16[16,4096]{1,0:T(8,128)(2,1)}), bf16[128,4096]{1,0:T(8,128)(2,1)}) %all-gather.2.cloned.1.call-update) | async-done | bytes 1048592 | tf_op jit(solution)/shard_map/all_gather | solution.py:125
  53.0 0.0 copy-start
  53.0 1.2 copy-done
  54.2 0.0 copy-start.1
  54.2 0.9 copy-done.1
  55.2 0.0 copy-start.2
  55.2 0.9 copy-done.2
  56.1 0.0 copy-start.3
  56.1 0.7 copy-done.3
  56.8 0.0 copy-start.4
  56.8 0.7 copy-done.4
  57.5 19.8 %local_sweep.1 = (f32[128,2048]{1,0:T(8,128)}, f32[128,4096]{1,0:T(8,128)}) custom-call(bf16[128,2048]{1,0:T(8,128)(2,1)S(1)} %all_gather.6.x_ref, bf16[128,4096]{1,0:T(8,128)(2,1)S(1)} %copy-done, f32[1,2048]{1,0:T(1,128)S(1)} %bitcast.3, f32[1,4096]{1,0:T(1,128)S(1)} %bitcast.2, f32[16,2048]{1,0:T(8,128)S(1)} %copy-done.2, f32[16,4096]{1,0:T(8,128)S(1)} %copy-done.1), custom_call_target="tpu_custom_call" | custom-call | tf_op jit(solution)/shard_map/local_sweep/pallas_call | solution.py:127
  77.3 0.0 reduce-scatter.3.cloned.1.call-update
  77.3 0.0 reduce-scatter.5.cloned.1.call-start
  77.4 0.7 reduce-scatter.5.cloned.1.call-update
  78.0 6.7 %reduce-scatter.3.cloned.1.call-done = f32[64,2048]{1,0:T(8,128)} async-done(((f32[128,2048]{1,0:T(8,128)}), f32[64,2048]{1,0:T(8,128)}) %reduce-scatter.3.cloned.1.call-update) | async-done | bytes 524304 | tf_op jit(solution)/shard_map/reduce_scatter | solution.py:148
  84.8 73.6 %reduce-scatter.5.cloned.1.call-done = f32[16,4096]{1,0:T(8,128)} async-done(((f32[128,4096]{1,0:T(8,128)}), f32[16,4096]{1,0:T(8,128)}) %reduce-scatter.5.cloned.1.call-update) | async-done | bytes 262160 | tf_op jit(solution)/shard_map/reduce_scatter | solution.py:147
Async XLA Ops:
  7.2 45.8 %all-gather.2.cloned.1.call-start = ((), (), s32[]{:S(2)}) async-start(), calls=%async_computation.2 | async-start | bytes 1179648 | tf_op jit(solution)/shard_map/all_gather | solution.py:125
  7.9 76.9 %reduce-scatter.3.cloned.1.call-start = ((), (), s32[]{:S(2)}) async-start(), calls=%async_computation.3 | async-start | bytes 1572864 | tf_op jit(solution)/shard_map/reduce_scatter | solution.py:148
  53.0 1.2 copy-start
  54.2 0.9 copy-start.1
  55.2 0.9 copy-start.2
  56.1 0.7 copy-start.3
  56.8 0.7 copy-start.4
  77.3 81.1 %reduce-scatter.5.cloned.1.call-start = ((), (), s32[]{:S(2)}) async-start(), calls=%async_computation.4 | async-start | bytes 2359296 | tf_op jit(solution)/shard_map/reduce_scatter | solution.py:147
Sparse Core Ops, SparseCore 0:
  10.1 42.8 all-gather.1
  77.4 7.2 reduce-scatter.2
  89.3 69.0 reduce-scatter.4

commit v2 on v1

--- a/solution.py
+++ b/solution.py
@@ -14,6 +14,7 @@
 STRIP = 512
 ROW_TILE = 256
 COL_TILE = 512
+AHEAD = 2
 LOG2E = 1.4426950408889634
 F32 = jnp.float32
 BF16 = jnp.bfloat16
@@ -149,9 +150,255 @@
     return (row_grad, col_grad)
 
 
+def fused_kernel(
+    pair_count, x_ref, z_ref, sr_ref, sc_ref, pr_ref, pc_ref, row_ref, col_ref,
+    x_aug, z_aug, x_turn, rw_turn, c_weight, row_acc, col_acc,
+    col_part, pair_send, pair_recv, line_send, line_recv, row_send, row_recv,
+    x_sems, own_send_sems, pass_send_sems, line_in, pair_in,
+    pair_send_sem, pair_sum_in, line_send_sems, line_sum_in, row_send_sem, row_in,
+):
+    inverse_sq = 4.0 / FEATURES
+    row_count, col_count = x_ref.shape[1], z_ref.shape[1]
+    x_rows, z_rows = x_ref.shape[0], z_ref.shape[0]
+    row_tiles, chunks = row_count // ROW_TILE, col_count // COL_TILE
+    others = pair_count - 1
+    me_row, me_col = lax.axis_index("row"), lax.axis_index("col")
+    side, place = lax.rem(me_row, 2), me_row // 2
+    pair_row = 2 * place + 1 - side
+    other_col = 1 - me_col
+
+    def line_place(step):
+        return lax.rem(place + step, pair_count)
+
+    def piece(owner, size):
+        return pl.ds(pl.multiple_of(owner * size, size), size)
+
+    def send(src, dst, send_sem, recv_sem, where):
+        return pltpu.make_async_remote_copy(
+            src_ref=src, dst_ref=dst, send_sem=send_sem, recv_sem=recv_sem,
+            device_id=where, device_id_type=pl.DeviceIdType.MESH,
+        )
+
+    barrier = pltpu.get_barrier_semaphore()
+    partners = [{"col": other_col}, {"row": pair_row}]
+    partners += [{"row": 2 * line_place(k) + side} for k in range(1, pair_count)]
+    for partner in partners:
+        pl.semaphore_signal(barrier, inc=1, device_id=partner, device_id_type=pl.DeviceIdType.MESH)
+    pl.semaphore_wait(barrier, len(partners))
+
+    my_x = piece(me_col, x_rows)
+    x_copy = send(x_ref, x_aug.at[my_x, :], x_sems.at[0], x_sems.at[1], {"col": other_col})
+    my_z = piece(me_row, z_rows)
+
+    def own_copy(k, at, recv_sem):
+        where = pair_row if k == 0 else 2 * line_place(k) + side
+        return send(z_ref.at[:, at], z_aug.at[my_z, at], own_send_sems.at[k], recv_sem, {"row": where})
+
+    def pass_copy(k, at, recv_sem):
+        owner = piece(2 * line_place(k) + side, z_rows)
+        return send(z_aug.at[owner, at], z_aug.at[owner, at], pass_send_sems.at[k - 1], recv_sem, {"row": pair_row})
+
+    @pl.loop(0, chunks)
+    def _(c):
+        at = window(c, COL_TILE)
+        for k in range(1, pair_count):
+            own_copy(k, at, line_in.at[c]).start()
+        own_copy(0, at, pair_in.at[c]).start()
+        @pl.when(c == 0)
+        def _():
+            x_copy.start()
+
+    def take_line(c):
+        at = window(c, COL_TILE)
+        got = z_aug.at[pl.ds(0, others * z_rows), at]
+        pltpu.make_async_copy(got, got, line_in.at[c]).wait()
+        for k in range(1, pair_count):
+            pass_copy(k, at, pair_in.at[c]).start()
+
+    def take_pair(c):
+        got = z_aug.at[pl.ds(0, pair_count * z_rows), window(c, COL_TILE)]
+        pltpu.make_async_copy(got, got, pair_in.at[c]).wait()
+
+    z_aug[my_z, :] = z_ref[...]
+    x_aug[my_x, :] = x_ref[...]
+
+    @pl.loop(0, row_count // STRIP)
+    def _(index_now):
+        at = window(index_now, STRIP)
+        rw_turn[at, :] = turned(weight_rows(sr_ref[:, at], pr_ref[:, at], 0.5, -0.5 / PROBES, False))
+
+    row_acc[...] = jnp.zeros_like(row_acc)
+    x_copy.wait_recv()
+
+    @pl.loop(0, row_count // STRIP)
+    def _(index_now):
+        at = window(index_now, STRIP)
+        x_aug[FEATURES:WIDE, at] = extra_rows(x_aug[0:FEATURES, at], False)
+        x_turn[at, :] = turned(x_aug[:, at])
+
+    for c in range(min(AHEAD, chunks)):
+        take_line(c)
+
+    def weighted_tile(i, at_j):
+        at_i = pl.ds(i * ROW_TILE, ROW_TILE)
+        half = jnp.dot(x_turn[at_i, :], z_aug[:, at_j], preferred_element_type=F32)
+        coupling = jnp.dot(rw_turn[at_i, :], c_weight[...], preferred_element_type=F32)
+        return (coupling * jnp.exp2(half * (inverse_sq * LOG2E))).astype(BF16)
+
+    def pair_copy(c):
+        return send(pair_send.at[c], pair_recv.at[c], pair_send_sem, pair_sum_in.at[c], {"row": pair_row})
+
+    def line_copy(c, k):
+        return send(
+            line_send.at[c, k - 1], line_recv.at[c, k - 1], line_send_sems.at[k - 1], line_sum_in.at[c],
+            {"row": 2 * line_place(k) + side},
+        )
+
+    def add_pair(c):
+        pltpu.make_async_copy(pair_recv.at[c], pair_recv.at[c], pair_sum_in.at[c]).wait()
+        for k in range(1, pair_count):
+            there = line_place(k)
+            total = col_part[c, piece(2 * there + side, z_rows), :] + pair_recv[c, there]
+            line_send[c, k - 1] = total
+            line_copy(c, k).start()
+
+    def add_line(c):
+        pltpu.make_async_copy(line_recv.at[c], line_recv.at[c], line_sum_in.at[c]).wait()
+        total = col_part[c, my_z, :] + pair_recv[c, place]
+        for k in range(1, pair_count):
+            total = total + line_recv[c, k - 1]
+        col_ref[:, window(c, COL_TILE)] = total
+
+    @pl.loop(0, chunks)
+    def _(c):
+        at_j = window(c, COL_TILE)
+
+        @pl.when(c + AHEAD < chunks)
+        def _():
+            take_line(c + AHEAD)
+
+        c_weight[...] = weight_rows(sc_ref[:, at_j], pc_ref[:, at_j], 1.0, 1.0, True)
+        take_pair(c)
+        z_aug[FEATURES:WIDE, at_j] = extra_rows(z_aug[0:FEATURES, at_j], True)
+        weighted = weighted_tile(0, at_j)
+        for i in range(row_tiles):
+            following = weighted_tile(i + 1, at_j) if i + 1 < row_tiles else None
+            at_i = pl.ds(i * ROW_TILE, ROW_TILE)
+            row_acc[:, at_i] += lax.dot_general(
+                z_aug[:, at_j], weighted, (((1,), (1,)), ((), ())), preferred_element_type=F32
+            )
+            part = jnp.dot(x_aug[:, at_i], weighted, preferred_element_type=F32)
+            if i == 0:
+                col_acc[...] = part
+            else:
+                col_acc[...] += part
+            weighted = following
+        col_part[c] = inverse_sq * (
+            col_acc[0:FEATURES, :] - z_aug[0:FEATURES, at_j].astype(F32) * col_acc[FEATURES:FEATURES + 1, :]
+        )
+        for there in range(pair_count):
+            pair_send[c, there] = col_part[c, piece(2 * there + 1 - side, z_rows), :]
+        pair_copy(c).start()
+
+        @pl.when(c >= 1)
+        def _():
+            add_pair(c - 1)
+
+    def row_piece(owner, at):
+        at_f = piece(owner, x_rows)
+        return inverse_sq * (
+            row_acc[at_f, at] - x_aug[at_f, at].astype(F32) * row_acc[FEATURES + 3:FEATURES + 4, at]
+        )
+
+    def row_copy(index_now):
+        return send(
+            row_send.at[index_now], row_recv.at[index_now], row_send_sem, row_in.at[index_now], {"col": other_col}
+        )
+
+    strips = row_count // STRIP
+
+    @pl.loop(0, strips)
+    def _(index_now):
+        row_send[index_now] = row_piece(other_col, window(index_now, STRIP))
+        row_copy(index_now).start()
+
+    add_pair(chunks - 1)
+
+    @pl.loop(0, chunks - 1)
+    def _(c):
+        add_line(c)
+
+    @pl.loop(0, strips)
+    def _(index_now):
+        at = window(index_now, STRIP)
+        row_copy(index_now).wait_recv()
+        row_ref[:, at] = row_piece(me_col, at) + row_recv[index_now]
+
+    add_line(chunks - 1)
+
+    x_copy.wait_send()
+    for k in range(pair_count):
+        own_copy(k, pl.ds(0, col_count), line_in.at[0]).wait_send()
+    for k in range(1, pair_count):
+        pass_copy(k, pl.ds(0, col_count), pair_in.at[0]).wait_send()
+        sent = line_send.at[:, k - 1]
+        pltpu.make_async_copy(sent, sent, line_send_sems.at[k - 1]).wait()
+    pltpu.make_async_copy(pair_send, pair_send, pair_send_sem).wait()
+    pltpu.make_async_copy(row_send, row_send, row_send_sem).wait()
+
+
+def fused_shards(rows, row_features, col_features, solve_rows, solve_cols, probe_rows, probe_cols):
+    (x_rows, row_count), (z_rows, col_count) = row_features.shape, col_features.shape
+    pair_count, chunks, strips = rows // 2, col_count // COL_TILE, row_count // STRIP
+    vmem = pl.BlockSpec(memory_space=pltpu.VMEM)
+    dma = pltpu.SemaphoreType.DMA
+    return pl.pallas_call(
+        functools.partial(fused_kernel, pair_count),
+        out_shape=(
+            jax.ShapeDtypeStruct((x_rows, row_count), F32),
+            jax.ShapeDtypeStruct((z_rows, col_count), F32),
+        ),
+        in_specs=[vmem] * 6,
+        out_specs=(vmem, vmem),
+        scratch_shapes=[
+            pltpu.VMEM((WIDE, row_count), BF16),
+            pltpu.VMEM((WIDE, col_count), BF16),
+            pltpu.VMEM((row_count, WIDE), BF16),
+            pltpu.VMEM((row_count, WEIGHT_ROWS), BF16),
+            pltpu.VMEM((WEIGHT_ROWS, COL_TILE), BF16),
+            pltpu.VMEM((WIDE, row_count), F32),
+            pltpu.VMEM((WIDE, COL_TILE), F32),
+            pltpu.VMEM((chunks, FEATURES, COL_TILE), F32),
+            pltpu.VMEM((chunks, pair_count, z_rows, COL_TILE), F32),
+            pltpu.VMEM((chunks, pair_count, z_rows, COL_TILE), F32),
+            pltpu.VMEM((chunks, pair_count - 1, z_rows, COL_TILE), F32),
+            pltpu.VMEM((chunks, pair_count - 1, z_rows, COL_TILE), F32),
+            pltpu.VMEM((strips, x_rows, STRIP), F32),
+            pltpu.VMEM((strips, x_rows, STRIP), F32),
+            dma((2,)),
+            dma((pair_count,)),
+            dma((pair_count - 1,)),
+            dma((chunks,)),
+            dma((chunks,)),
+            dma,
+            dma((chunks,)),
+            dma((pair_count - 1,)),
+            dma((chunks,)),
+            dma,
+            dma((strips,)),
+        ],
+        compiler_params=pltpu.CompilerParams(
+            collective_id=0, has_side_effects=True, vmem_limit_bytes=48 * 2**20
+        ),
+        name="fused_sweep",
+    )(row_features, col_features, solve_rows[None, :], solve_cols[None, :], probe_rows, probe_cols)
+
+
 def solution(mesh):
+    rows = mesh.shape["row"]
+    whole_tiles = (FEATURES // rows) % 16 == 0 and rows >= 4 and rows % 2 == 0 and mesh.shape["col"] == 2
     return jax.shard_map(
-        shards,
+        functools.partial(fused_shards, rows) if whole_tiles else shards,
         mesh=mesh,
         in_specs=(
             P("col", ("pool", "row")),

time: 165 us -> 56.9 us (0.34)
  waiting for transfers between devices: 124 us -> 0 us
  Pallas kernels: 19.8 us -> 49.4 us
  between operations: 13.7 us -> 0.65 us
  blocking collectives: 2.47 us -> 0 us
  local copies, waits for them, and re-layouts: 4.49 us -> 6.61 us
    reduce_scatter x2 -> x0, waiting for transfers between devices: 80.3 us -> none  [the longest x1 73.6 us: shards(): lax.psum_scatter(col_part, 'row', scatter_dimension=0, tiled=True)]
    all_gather x1 -> x0, waiting for transfers between devices: 42.6 us -> none  [shards(): col_full = lax.all_gather(col_features, 'row', axis=0, tiled=True)]
    pallas_call x1, Pallas kernels: 19.8 us -> 49.4 us  [fused_shards(): pl.pallas_call(functools.partial(fused_kernel, pair_count), out_shape=(ja...]
    all_gather x1 -> x0, blocking collectives: 2.47 us -> none  [shards(): row_full = lax.all_gather(row_features, 'col', axis=0, tiled=True)]
    unnamed x10 -> x14, local copies, waits for them, and re-layouts: 4.49 us -> 6.61 us
  transfers between devices with their start and end apart: 3 -> 0, of which waited for: 3 -> 0; matrix products, arithmetic and copies ran while one was open for 0% -> 0% of each run, Pallas kernels for 0% -> 0%
where the time goes in v2:
time: 56.9 us; the launch traced here: 56.6 us
  Pallas kernels  49.4 us (87%)
  local copies, waits for them, and re-layouts  6.61 us (12%)
  between operations  0.65 us (1%)
    pallas_call x1, Pallas kernels, fused_shards(): pl.pallas_call(functools.partial(fused_kernel, pair_count), out_shape=(ja...  49.4 us
    unnamed x14, local copies, waits for them, and re-layouts  6.61 us

profile of v2, /device:TPU:0, one launch (start us, length us, event | category | flops | bytes accessed | tf_op | source)
XLA Modules:
  0.0 56.6 jit_solution(8738875053026786505)
XLA Ops:
  0.6 0.0 copy-start
  0.6 0.9 %copy-done = bf16[64,2048]{1,0:T(8,128)(2,1)S(1)} copy-done((bf16[64,2048]{1,0:T(8,128)(2,1)S(1)}, bf16[64,2048]{1,0:T(8,128)(2,1)}, u32[]{:S(2)}) %copy-start) | copy-done | bytes 262168
  1.6 0.0 copy-start.1
  1.6 0.9 %copy-done.1 = f32[16,4096]{1,0:T(8,128)S(1)} copy-done((f32[16,4096]{1,0:T(8,128)S(1)}, f32[16,4096]{1,0:T(8,128)}, u32[]{:S(2)}) %copy-start.1) | copy-done | bytes 262168
  2.5 0.0 copy-start.2
  2.5 0.9 %copy-done.2 = bf16[16,4096]{1,0:T(8,128)(2,1)S(1)} copy-done((bf16[16,4096]{1,0:T(8,128)(2,1)S(1)}, bf16[16,4096]{1,0:T(8,128)(2,1)}, u32[]{:S(2)}) %copy-start.2) | copy-done | bytes 131096
  3.4 0.0 copy-start.3
  3.4 0.9 %copy-done.3 = f32[16,2048]{1,0:T(8,128)S(1)} copy-done((f32[16,2048]{1,0:T(8,128)S(1)}, f32[16,2048]{1,0:T(8,128)}, u32[]{:S(2)}) %copy-start.3) | copy-done | bytes 131096
  4.3 0.0 copy-start.4
  4.3 0.7 %copy-done.4 = f32[4096]{0:T(1024)S(1)} copy-done((f32[4096]{0:T(1024)S(1)}, f32[4096]{0:T(1024)}, u32[]{:S(2)}) %copy-start.4) | copy-done | bytes 16408
  5.1 0.0 copy-start.5
  5.1 0.7 %copy-done.5 = f32[2048]{0:T(1024)S(1)} copy-done((f32[2048]{0:T(1024)S(1)}, f32[2048]{0:T(1024)}, u32[]{:S(2)}) %copy-start.5) | copy-done | bytes 8216
  5.8 49.4 %fused_sweep.1 = (f32[64,2048]{1,0:T(8,128)S(1)}, f32[16,4096]{1,0:T(8,128)S(1)}) custom-call(bf16[64,2048]{1,0:T(8,128)(2,1)S(1)} %copy-done, bf16[16,4096]{1,0:T(8,128)(2,1)S(1)} %copy-done.2, f32[1,2048]{1,0:T(1,128)S(1)} %bitcast.3, f32[1,4096]{1,0:T(1,128)S(1)} %bitcast.2, f32[16,2048]{1,0:T(8,128)S(1)} %copy-done.3, f32[16,4096]{1,0:T(8,128)S(1)} %copy-done.1), custom_call_target="tpu_custom_call" | custom-call | tf_op jit(solution)/shard_map/fused_sweep/pallas_call | solution.py:355
  55.1 0.8 %copy.10 = f32[64,2048]{1,0:T(8,128)} copy(f32[64,2048]{1,0:T(8,128)S(1)} %get-tuple-element.4) | data formatting | bytes 1048576
  55.9 0.7 %copy.11 = f32[16,4096]{1,0:T(8,128)} copy(f32[16,4096]{1,0:T(8,128)S(1)} %get-tuple-element.5) | data formatting | bytes 524288
Async XLA Ops:
  0.6 1.0 %copy-start = (bf16[64,2048]{1,0:T(8,128)(2,1)S(1)}, bf16[64,2048]{1,0:T(8,128)(2,1)}, u32[]{:S(2)}) copy-start(bf16[64,2048]{1,0:T(8,128)(2,1)} %x_ref.1) | copy-start | bytes 786436
  1.6 0.9 %copy-start.1 = (f32[16,4096]{1,0:T(8,128)S(1)}, f32[16,4096]{1,0:T(8,128)}, u32[]{:S(2)}) copy-start(f32[16,4096]{1,0:T(8,128)} %pc_ref.1) | copy-start | bytes 786436
  2.5 0.9 %copy-start.2 = (bf16[16,4096]{1,0:T(8,128)(2,1)S(1)}, bf16[16,4096]{1,0:T(8,128)(2,1)}, u32[]{:S(2)}) copy-start(bf16[16,4096]{1,0:T(8,128)(2,1)} %z_ref.1) | copy-start | bytes 393220
  3.4 0.9 %copy-start.3 = (f32[16,2048]{1,0:T(8,128)S(1)}, f32[16,2048]{1,0:T(8,128)}, u32[]{:S(2)}) copy-start(f32[16,2048]{1,0:T(8,128)} %pr_ref.1) | copy-start | bytes 393220
  4.3 0.7 %copy-start.4 = (f32[4096]{0:T(1024)S(1)}, f32[4096]{0:T(1024)}, u32[]{:S(2)}) copy-start(f32[4096]{0:T(1024)} %param.9) | copy-start | bytes 49156
  5.1 0.7 %copy-start.5 = (f32[2048]{0:T(1024)S(1)}, f32[2048]{0:T(1024)}, u32[]{:S(2)}) copy-start(f32[2048]{0:T(1024)} %param.8) | copy-start | bytes 24580

commit v3 on v2

--- a/solution.py
+++ b/solution.py
@@ -13,8 +13,9 @@
 WEIGHT_ROWS = 64
 STRIP = 512
 ROW_TILE = 256
-COL_TILE = 512
+COL_TILE = 1024
 AHEAD = 2
+SCALE_LANES = 128
 LOG2E = 1.4426950408889634
 F32 = jnp.float32
 BF16 = jnp.bfloat16
@@ -150,12 +151,31 @@
     return (row_grad, col_grad)
 
 
+def encode(values):
+    peak = jnp.max(jnp.max(jnp.abs(values), 0, keepdims=True), 1, keepdims=True)
+    scale = jnp.maximum(peak, 1e-35).astype(BF16).astype(F32)
+    ratio = values * (1.0 / scale)
+    square = ratio * ratio
+    coded = square * square * square * ratio
+    lanes = jnp.broadcast_to(scale, (values.shape[0], SCALE_LANES))
+    return coded.astype(BF16), lanes.astype(BF16)
+
+
+def decode(block):
+    wide = block.astype(F32)
+    coded, scale = wide[:, 0:COL_TILE], wide[:, COL_TILE:COL_TILE + 1]
+    size = jnp.abs(coded)
+    root = jnp.exp2(jnp.log(jnp.maximum(size, 1e-37)) * (LOG2E / 7.0)) * scale
+    return jnp.where(size < 1e-37, 0.0, jnp.where(coded < 0.0, -root, root))
+
+
 def fused_kernel(
     pair_count, x_ref, z_ref, sr_ref, sc_ref, pr_ref, pc_ref, row_ref, col_ref,
     x_aug, z_aug, x_turn, rw_turn, c_weight, row_acc, col_acc,
     col_part, pair_send, pair_recv, line_send, line_recv, row_send, row_recv,
     x_sems, own_send_sems, pass_send_sems, line_in, pair_in,
     pair_send_sem, pair_sum_in, line_send_sems, line_sum_in, row_send_sem, row_in,
+    pr_held, pc_held, load_sems,
 ):
     inverse_sq = 4.0 / FEATURES
     row_count, col_count = x_ref.shape[1], z_ref.shape[1]
@@ -219,15 +239,24 @@
         got = z_aug.at[pl.ds(0, pair_count * z_rows), window(c, COL_TILE)]
         pltpu.make_async_copy(got, got, pair_in.at[c]).wait()
 
-    z_aug[my_z, :] = z_ref[...]
-    x_aug[my_x, :] = x_ref[...]
+    loads = [
+        pltpu.make_async_copy(src, dst, load_sems.at[n])
+        for n, (src, dst) in enumerate(
+            [(pr_ref, pr_held), (x_ref, x_aug.at[my_x, :]), (z_ref, z_aug.at[my_z, :]), (pc_ref, pc_held)]
+        )
+    ]
+    for load in loads:
+        load.start()
+    loads[0].wait()
 
     @pl.loop(0, row_count // STRIP)
     def _(index_now):
         at = window(index_now, STRIP)
-        rw_turn[at, :] = turned(weight_rows(sr_ref[:, at], pr_ref[:, at], 0.5, -0.5 / PROBES, False))
+        rw_turn[at, :] = turned(weight_rows(sr_ref[:, at], pr_held[:, at], 0.5, -0.5 / PROBES, False))
 
     row_acc[...] = jnp.zeros_like(row_acc)
+    for load in loads[1:]:
+        load.wait()
     x_copy.wait_recv()
 
     @pl.loop(0, row_count // STRIP)
@@ -258,15 +287,17 @@
         pltpu.make_async_copy(pair_recv.at[c], pair_recv.at[c], pair_sum_in.at[c]).wait()
         for k in range(1, pair_count):
             there = line_place(k)
-            total = col_part[c, piece(2 * there + side, z_rows), :] + pair_recv[c, there]
-            line_send[c, k - 1] = total
+            total = col_part[c, piece(2 * there + side, z_rows), :] + decode(pair_recv[c, there])
+            coded, scale = encode(total)
+            line_send[c, k - 1, :, 0:COL_TILE] = coded
+            line_send[c, k - 1, :, COL_TILE:COL_TILE + SCALE_LANES] = scale
             line_copy(c, k).start()
 
     def add_line(c):
         pltpu.make_async_copy(line_recv.at[c], line_recv.at[c], line_sum_in.at[c]).wait()
-        total = col_part[c, my_z, :] + pair_recv[c, place]
+        total = col_part[c, my_z, :] + decode(pair_recv[c, place])
         for k in range(1, pair_count):
-            total = total + line_recv[c, k - 1]
+            total = total + decode(line_recv[c, k - 1])
         col_ref[:, window(c, COL_TILE)] = total
 
     @pl.loop(0, chunks)
@@ -277,7 +308,7 @@
         def _():
             take_line(c + AHEAD)
 
-        c_weight[...] = weight_rows(sc_ref[:, at_j], pc_ref[:, at_j], 1.0, 1.0, True)
+        c_weight[...] = weight_rows(sc_ref[:, at_j], pc_held[:, at_j], 1.0, 1.0, True)
         take_pair(c)
         z_aug[FEATURES:WIDE, at_j] = extra_rows(z_aug[0:FEATURES, at_j], True)
         weighted = weighted_tile(0, at_j)
@@ -297,7 +328,9 @@
             col_acc[0:FEATURES, :] - z_aug[0:FEATURES, at_j].astype(F32) * col_acc[FEATURES:FEATURES + 1, :]
         )
         for there in range(pair_count):
-            pair_send[c, there] = col_part[c, piece(2 * there + 1 - side, z_rows), :]
+            coded, scale = encode(col_part[c, piece(2 * there + 1 - side, z_rows), :])
+            pair_send[c, there, :, 0:COL_TILE] = coded
+            pair_send[c, there, :, COL_TILE:COL_TILE + SCALE_LANES] = scale
         pair_copy(c).start()
 
         @pl.when(c >= 1)
@@ -350,7 +383,7 @@
 def fused_shards(rows, row_features, col_features, solve_rows, solve_cols, probe_rows, probe_cols):
     (x_rows, row_count), (z_rows, col_count) = row_features.shape, col_features.shape
     pair_count, chunks, strips = rows // 2, col_count // COL_TILE, row_count // STRIP
-    vmem = pl.BlockSpec(memory_space=pltpu.VMEM)
+    vmem, hbm = pl.BlockSpec(memory_space=pltpu.VMEM), pl.BlockSpec(memory_space=pl.ANY)
     dma = pltpu.SemaphoreType.DMA
     return pl.pallas_call(
         functools.partial(fused_kernel, pair_count),
@@ -358,7 +391,7 @@
             jax.ShapeDtypeStruct((x_rows, row_count), F32),
             jax.ShapeDtypeStruct((z_rows, col_count), F32),
         ),
-        in_specs=[vmem] * 6,
+        in_specs=[hbm, hbm, vmem, vmem, hbm, hbm],
         out_specs=(vmem, vmem),
         scratch_shapes=[
             pltpu.VMEM((WIDE, row_count), BF16),
@@ -369,10 +402,10 @@
             pltpu.VMEM((WIDE, row_count), F32),
             pltpu.VMEM((WIDE, COL_TILE), F32),
             pltpu.VMEM((chunks, FEATURES, COL_TILE), F32),
-            pltpu.VMEM((chunks, pair_count, z_rows, COL_TILE), F32),
-            pltpu.VMEM((chunks, pair_count, z_rows, COL_TILE), F32),
-            pltpu.VMEM((chunks, pair_count - 1, z_rows, COL_TILE), F32),
-            pltpu.VMEM((chunks, pair_count - 1, z_rows, COL_TILE), F32),
+            pltpu.VMEM((chunks, pair_count, z_rows, COL_TILE + SCALE_LANES), BF16),
+            pltpu.VMEM((chunks, pair_count, z_rows, COL_TILE + SCALE_LANES), BF16),
+            pltpu.VMEM((chunks, pair_count - 1, z_rows, COL_TILE + SCALE_LANES), BF16),
+            pltpu.VMEM((chunks, pair_count - 1, z_rows, COL_TILE + SCALE_LANES), BF16),
             pltpu.VMEM((strips, x_rows, STRIP), F32),
             pltpu.VMEM((strips, x_rows, STRIP), F32),
             dma((2,)),
@@ -386,6 +419,9 @@
             dma((chunks,)),
             dma,
             dma((strips,)),
+            pltpu.VMEM((PROBES, row_count), F32),
+            pltpu.VMEM((PROBES, col_count), F32),
+            dma((4,)),
         ],
         compiler_params=pltpu.CompilerParams(
             collective_id=0, has_side_effects=True, vmem_limit_bytes=48 * 2**20

time: 56.9 us -> 52.9 us (0.930)
  Pallas kernels: 49.4 us -> 45.4 us
    pallas_call x1, Pallas kernels: 49.4 us -> 45.4 us  [fused_shards(): pl.pallas_call(functools.partial(fused_kernel, pair_count), out_shape=(ja...]
where the time goes in v3:
time: 52.9 us; the launch traced here: 52.6 us
  Pallas kernels  45.4 us (86%)
  local copies, waits for them, and re-layouts  6.61 us (12%)
  between operations  0.65 us (1%)
    pallas_call x1, Pallas kernels, fused_shards(): pl.pallas_call(functools.partial(fused_kernel, pair_count), out_shape=(ja...  45.4 us
    unnamed x14, local copies, waits for them, and re-layouts  6.61 us

profile of v3, /device:TPU:0, one launch (start us, length us, event | category | flops | bytes accessed | tf_op | source)
XLA Modules:
  0.0 52.6 jit_solution(6737698240640021503)
XLA Ops:
  0.6 0.0 copy-start
  0.6 0.9 %copy-done = bf16[64,2048]{1,0:T(8,128)(2,1)S(1)} copy-done((bf16[64,2048]{1,0:T(8,128)(2,1)S(1)}, bf16[64,2048]{1,0:T(8,128)(2,1)}, u32[]{:S(2)}) %copy-start) | copy-done | bytes 262168
  1.6 0.0 copy-start.1
  1.6 0.9 %copy-done.1 = f32[16,4096]{1,0:T(8,128)S(1)} copy-done((f32[16,4096]{1,0:T(8,128)S(1)}, f32[16,4096]{1,0:T(8,128)}, u32[]{:S(2)}) %copy-start.1) | copy-done | bytes 262168
  2.5 0.0 copy-start.2
  2.5 0.9 %copy-done.2 = bf16[16,4096]{1,0:T(8,128)(2,1)S(1)} copy-done((bf16[16,4096]{1,0:T(8,128)(2,1)S(1)}, bf16[16,4096]{1,0:T(8,128)(2,1)}, u32[]{:S(2)}) %copy-start.2) | copy-done | bytes 131096
  3.4 0.0 copy-start.3
  3.4 0.9 %copy-done.3 = f32[16,2048]{1,0:T(8,128)S(1)} copy-done((f32[16,2048]{1,0:T(8,128)S(1)}, f32[16,2048]{1,0:T(8,128)}, u32[]{:S(2)}) %copy-start.3) | copy-done | bytes 131096
  4.3 0.0 copy-start.4
  4.3 0.7 %copy-done.4 = f32[4096]{0:T(1024)S(1)} copy-done((f32[4096]{0:T(1024)S(1)}, f32[4096]{0:T(1024)}, u32[]{:S(2)}) %copy-start.4) | copy-done | bytes 16408
  5.1 0.0 copy-start.5
  5.1 0.7 %copy-done.5 = f32[2048]{0:T(1024)S(1)} copy-done((f32[2048]{0:T(1024)S(1)}, f32[2048]{0:T(1024)}, u32[]{:S(2)}) %copy-start.5) | copy-done | bytes 8216
  5.8 45.4 %fused_sweep.1 = (f32[64,2048]{1,0:T(8,128)S(1)}, f32[16,4096]{1,0:T(8,128)S(1)}) custom-call(bf16[64,2048]{1,0:T(8,128)(2,1)S(1)} %copy-done, bf16[16,4096]{1,0:T(8,128)(2,1)S(1)} %copy-done.2, f32[1,2048]{1,0:T(1,128)S(1)} %bitcast.3, f32[1,4096]{1,0:T(1,128)S(1)} %bitcast.2, f32[16,2048]{1,0:T(8,128)S(1)} %copy-done.3, f32[16,4096]{1,0:T(8,128)S(1)} %copy-done.1), custom_call_target="tpu_custom_call" | custom-call | tf_op jit(solution)/shard_map/fused_sweep/pallas_call | solution.py:388
  51.1 0.8 %copy.10 = f32[64,2048]{1,0:T(8,128)} copy(f32[64,2048]{1,0:T(8,128)S(1)} %get-tuple-element.4) | data formatting | bytes 1048576
  51.9 0.7 %copy.11 = f32[16,4096]{1,0:T(8,128)} copy(f32[16,4096]{1,0:T(8,128)S(1)} %get-tuple-element.5) | data formatting | bytes 524288
Async XLA Ops:
  0.6 1.0 %copy-start = (bf16[64,2048]{1,0:T(8,128)(2,1)S(1)}, bf16[64,2048]{1,0:T(8,128)(2,1)}, u32[]{:S(2)}) copy-start(bf16[64,2048]{1,0:T(8,128)(2,1)} %x_ref.1) | copy-start | bytes 786436
  1.6 0.9 %copy-start.1 = (f32[16,4096]{1,0:T(8,128)S(1)}, f32[16,4096]{1,0:T(8,128)}, u32[]{:S(2)}) copy-start(f32[16,4096]{1,0:T(8,128)} %pc_ref.1) | copy-start | bytes 786436
  2.5 0.9 %copy-start.2 = (bf16[16,4096]{1,0:T(8,128)(2,1)S(1)}, bf16[16,4096]{1,0:T(8,128)(2,1)}, u32[]{:S(2)}) copy-start(bf16[16,4096]{1,0:T(8,128)(2,1)} %z_ref.1) | copy-start | bytes 393220
  3.4 0.9 %copy-start.3 = (f32[16,2048]{1,0:T(8,128)S(1)}, f32[16,2048]{1,0:T(8,128)}, u32[]{:S(2)}) copy-start(f32[16,2048]{1,0:T(8,128)} %pr_ref.1) | copy-start | bytes 393220
  4.3 0.7 %copy-start.4 = (f32[4096]{0:T(1024)S(1)}, f32[4096]{0:T(1024)}, u32[]{:S(2)}) copy-start(f32[4096]{0:T(1024)} %param.9) | copy-start | bytes 49156
  5.1 0.7 %copy-start.5 = (f32[2048]{0:T(1024)S(1)}, f32[2048]{0:T(1024)}, u32[]{:S(2)}) copy-start(f32[2048]{0:T(1024)} %param.8) | copy-start | bytes 24580

commit v4 on v3

--- a/solution.py
+++ b/solution.py
@@ -254,6 +254,7 @@
         at = window(index_now, STRIP)
         rw_turn[at, :] = turned(weight_rows(sr_ref[:, at], pr_held[:, at], 0.5, -0.5 / PROBES, False))
 
+    take_line(0)
     row_acc[...] = jnp.zeros_like(row_acc)
     for load in loads[1:]:
         load.wait()
@@ -265,7 +266,7 @@
         x_aug[FEATURES:WIDE, at] = extra_rows(x_aug[0:FEATURES, at], False)
         x_turn[at, :] = turned(x_aug[:, at])
 
-    for c in range(min(AHEAD, chunks)):
+    for c in range(1, min(AHEAD, chunks)):
         take_line(c)
 
     def weighted_tile(i, at_j):

time: 52.9 us -> 52.9 us (level)
  no operation moved by 1% of the time
where the time goes in v4:
time: 52.9 us; the launch traced here: 52.6 us
  Pallas kernels  45.4 us (86%)
  local copies, waits for them, and re-layouts  6.61 us (12%)
  between operations  0.65 us (1%)
    pallas_call x1, Pallas kernels, fused_shards(): pl.pallas_call(functools.partial(fused_kernel, pair_count), out_shape=(ja...  45.4 us
    unnamed x14, local copies, waits for them, and re-layouts  6.61 us

profile of v4, /device:TPU:0, one launch (start us, length us, event | category | flops | bytes accessed | tf_op | source)
XLA Modules:
  0.0 52.6 jit_solution(10010893320990063866)
XLA Ops:
  0.6 0.0 copy-start
  0.6 0.9 %copy-done = bf16[64,2048]{1,0:T(8,128)(2,1)S(1)} copy-done((bf16[64,2048]{1,0:T(8,128)(2,1)S(1)}, bf16[64,2048]{1,0:T(8,128)(2,1)}, u32[]{:S(2)}) %copy-start) | copy-done | bytes 262168
  1.6 0.0 copy-start.1
  1.6 0.9 %copy-done.1 = f32[16,4096]{1,0:T(8,128)S(1)} copy-done((f32[16,4096]{1,0:T(8,128)S(1)}, f32[16,4096]{1,0:T(8,128)}, u32[]{:S(2)}) %copy-start.1) | copy-done | bytes 262168
  2.5 0.0 copy-start.2
  2.5 0.9 %copy-done.2 = bf16[16,4096]{1,0:T(8,128)(2,1)S(1)} copy-done((bf16[16,4096]{1,0:T(8,128)(2,1)S(1)}, bf16[16,4096]{1,0:T(8,128)(2,1)}, u32[]{:S(2)}) %copy-start.2) | copy-done | bytes 131096
  3.4 0.0 copy-start.3
  3.4 0.9 %copy-done.3 = f32[16,2048]{1,0:T(8,128)S(1)} copy-done((f32[16,2048]{1,0:T(8,128)S(1)}, f32[16,2048]{1,0:T(8,128)}, u32[]{:S(2)}) %copy-start.3) | copy-done | bytes 131096
  4.3 0.0 copy-start.4
  4.3 0.7 %copy-done.4 = f32[4096]{0:T(1024)S(1)} copy-done((f32[4096]{0:T(1024)S(1)}, f32[4096]{0:T(1024)}, u32[]{:S(2)}) %copy-start.4) | copy-done | bytes 16408
  5.1 0.0 copy-start.5
  5.1 0.7 %copy-done.5 = f32[2048]{0:T(1024)S(1)} copy-done((f32[2048]{0:T(1024)S(1)}, f32[2048]{0:T(1024)}, u32[]{:S(2)}) %copy-start.5) | copy-done | bytes 8216
  5.8 45.4 %fused_sweep.1 = (f32[64,2048]{1,0:T(8,128)S(1)}, f32[16,4096]{1,0:T(8,128)S(1)}) custom-call(bf16[64,2048]{1,0:T(8,128)(2,1)S(1)} %copy-done, bf16[16,4096]{1,0:T(8,128)(2,1)S(1)} %copy-done.2, f32[1,2048]{1,0:T(1,128)S(1)} %bitcast.3, f32[1,4096]{1,0:T(1,128)S(1)} %bitcast.2, f32[16,2048]{1,0:T(8,128)S(1)} %copy-done.3, f32[16,4096]{1,0:T(8,128)S(1)} %copy-done.1), custom_call_target="tpu_custom_call" | custom-call | tf_op jit(solution)/shard_map/fused_sweep/pallas_call | solution.py:389
  51.1 0.8 %copy.10 = f32[64,2048]{1,0:T(8,128)} copy(f32[64,2048]{1,0:T(8,128)S(1)} %get-tuple-element.4) | data formatting | bytes 1048576
  51.9 0.7 %copy.11 = f32[16,4096]{1,0:T(8,128)} copy(f32[16,4096]{1,0:T(8,128)S(1)} %get-tuple-element.5) | data formatting | bytes 524288
Async XLA Ops:
  0.6 1.0 %copy-start = (bf16[64,2048]{1,0:T(8,128)(2,1)S(1)}, bf16[64,2048]{1,0:T(8,128)(2,1)}, u32[]{:S(2)}) copy-start(bf16[64,2048]{1,0:T(8,128)(2,1)} %x_ref.1) | copy-start | bytes 786436
  1.6 0.9 %copy-start.1 = (f32[16,4096]{1,0:T(8,128)S(1)}, f32[16,4096]{1,0:T(8,128)}, u32[]{:S(2)}) copy-start(f32[16,4096]{1,0:T(8,128)} %pc_ref.1) | copy-start | bytes 786436
  2.5 0.9 %copy-start.2 = (bf16[16,4096]{1,0:T(8,128)(2,1)S(1)}, bf16[16,4096]{1,0:T(8,128)(2,1)}, u32[]{:S(2)}) copy-start(bf16[16,4096]{1,0:T(8,128)(2,1)} %z_ref.1) | copy-start | bytes 393220
  3.4 0.9 %copy-start.3 = (f32[16,2048]{1,0:T(8,128)S(1)}, f32[16,2048]{1,0:T(8,128)}, u32[]{:S(2)}) copy-start(f32[16,2048]{1,0:T(8,128)} %pr_ref.1) | copy-start | bytes 393220
  4.3 0.7 %copy-start.4 = (f32[4096]{0:T(1024)S(1)}, f32[4096]{0:T(1024)}, u32[]{:S(2)}) copy-start(f32[4096]{0:T(1024)} %param.9) | copy-start | bytes 49156
  5.1 0.7 %copy-start.5 = (f32[2048]{0:T(1024)S(1)}, f32[2048]{0:T(1024)}, u32[]{:S(2)}) copy-start(f32[2048]{0:T(1024)} %param.8) | copy-start | bytes 24580
